TPU v7x, 256 devices: a whole 4x4x8 slice. The times are simulated.
256 devices in a mesh: space: 32 (over z_lo, y, core), fac: 8 (over z_hi, x).
Axes of the slice: x: 4, y: 4, z: 8 (z_hi: 2, z_lo: 4; z = z_hi * 4 + z_lo), core: 2. Of those that a mesh axis runs over, the one named last changes fastest.
Arguments:
- activations: bfloat16 [8, 64, 16, 16, 128], P('fac', 'space'), may hold values from -60 to 60
- out_grad: bfloat16 [8, 64, 16, 16, 128], P('fac', 'space'), may hold values from -60 to 60
- kernel: bfloat16 [27, 128, 128], replicated, may hold values from -0.109375 to 0.109375
Outputs:
- in_grad: bfloat16 [8, 64, 16, 16, 128], P('fac', 'space')
- update: float32 [27, 128, 128], P(None, 'fac')
All inputs are finite; a program needn't handle non-finite values.
Results may differ from a plain program's by a relative error of at most 0.0014.
Values may be sent and summed in bfloat16 or wider, within the bound.
No kernel may reach another device: no remote copies, remote signals or barrier semaphores. Data moves between devices by JAX's collectives and lax.ppermute only.
A program may use at most 128 MiB of HBM per device.

v0:
```python
import math
import jax
import jax.numpy as jnp
from jax import lax
from jax.sharding import PartitionSpec as P

damping = 0.1
clip_rate = 0.05


def with_halo(cells, sides, width):
    for axis, dim in sides:
        count = lax.axis_size(axis)
        ends = count - 1
        head = lax.slice_in_dim(cells, 0, width, axis=dim)
        tail = lax.slice_in_dim(cells, cells.shape[dim] - width, cells.shape[dim], axis=dim)
        cells = jnp.concatenate(
            [
                lax.ppermute(tail, axis, [(i, (i + 1) % count) for i in range(ends)]),
                cells,
                lax.ppermute(head, axis, [((i + 1) % count, i) for i in range(ends)]),
            ],
            axis=dim,
        )
    return cells


def offsets():
    return [(a, b, c) for a in (-1, 0, 1) for b in (-1, 0, 1) for c in (-1, 0, 1)]


def window(padded, shift, extent):
    return padded[
        1 + shift[0] : 1 + shift[0] + extent[0],
        1 + shift[1] : 1 + shift[1] + extent[1],
        1 + shift[2] : 1 + shift[2] + extent[2],
    ]


def local_stats(padded_in, rows_cot, extent, groups):
    cells = rows_cot.shape[0]
    width = padded_in.shape[-1] // groups
    gram_list = []
    grad_list = []
    for block_index in range(groups):
        lower = block_index * width
        pieces = [
            window(padded_in, shift, extent)[..., lower : lower + width].reshape(cells, width)
            for shift in offsets()
        ]
        patch = jnp.concatenate(pieces, axis=1)
        gram_list.append(jnp.dot(patch.T, patch, preferred_element_type=jnp.float32))
        grad_list.append(jnp.dot(patch.T, rows_cot, preferred_element_type=jnp.float32))
    grads = jnp.stack(grad_list)
    return (jnp.stack(gram_list), grads)


def on_device(activations, out_grad, kernel):
    inputs = activations[0]
    cotangent = out_grad[0]
    size_x, size_y, size_z, channels = inputs.shape
    extent = (size_x, size_y, size_z)
    cells = size_x * size_y * size_z
    groups = lax.axis_size("fac")
    width = channels // groups
    stacked = jnp.concatenate([inputs, cotangent], axis=3)
    rimmed = with_halo(stacked, (("space", 0),), 1)
    padded = jnp.pad(rimmed, ((0, 0), (1, 1), (1, 1), (0, 0)))
    padded_in = padded[..., :channels]
    padded_cot = padded[..., channels:]
    rows_cot = cotangent.reshape(cells, channels)
    cot_gram = jnp.dot(rows_cot.T, rows_cot, preferred_element_type=jnp.float32)
    in_grad = jnp.zeros((cells, channels), jnp.float32)
    for tap_index, shift in enumerate(offsets()):
        back = (-shift[0], -shift[1], -shift[2])
        rows = window(padded_cot, back, extent).reshape(cells, channels)
        in_grad = in_grad + jnp.dot(rows, kernel[tap_index].T, preferred_element_type=jnp.float32)
    in_grad = in_grad.astype(jnp.bfloat16).reshape(activations.shape)
    cot_total = lax.psum(cot_gram, ("space", "fac"))
    grams, grads = local_stats(padded_in, rows_cot, extent, groups)
    summed = lax.psum((grams, grads), "space")
    owned = (
        lax.psum_scatter(summed[0], "fac", scatter_dimension=0, tiled=True),
        lax.psum_scatter(summed[1], "fac", scatter_dimension=0, tiled=True),
    )
    gram_block = owned[0][0]
    grad_block = owned[1][0]
    count = float(cells * lax.axis_size("space") * groups)
    order = gram_block.shape[0]
    right_mat = cot_total / count + damping * jnp.eye(channels, dtype=jnp.float32)
    right_chol = jnp.linalg.cholesky(right_mat)
    left_mat = gram_block / count + damping * jnp.eye(order, dtype=jnp.float32)
    left_chol = jnp.linalg.cholesky(left_mat)
    scaled = grad_block / math.sqrt(count)
    half = jax.scipy.linalg.cho_solve((left_chol, True), scaled)
    raw = jax.scipy.linalg.cho_solve((right_chol, True), half.T).T
    total = lax.psum(jnp.sum(raw * scaled), "fac")
    factor = jnp.sqrt(clip_rate * kernel.size / total)
    update = raw.reshape(27, width, channels) * factor
    return (in_grad, update)


def solution(mesh):
    placed = (P("fac", "space", None, None, None), P("fac", "space", None, None, None), P())
    return jax.shard_map(
        on_device,
        mesh=mesh,
        in_specs=placed,
        out_specs=(P("fac", "space", None, None, None), P(None, "fac", None)),
        check_vma=False,
    )
```

profile of v0, /device:TPU:0, one launch (start us, length us, event | category | flops | bytes accessed | tf_op | source)
XLA Modules:
  0.0 795.9 jit_solution(12100450884241944340)
XLA Ops:
  8.1 1.9 convolution_bitcast_fusion.16
  16.7 1.6 fusion.150
  18.4 1.7 fusion.154
  20.1 2.2 fusion.152
  22.3 2.3 fusion.148
  24.6 2.3 fusion.149
  26.9 2.2 fusion.146
  29.1 2.2 fusion.153
  31.3 2.3 fusion.147
  33.6 2.2 fusion.151
  35.8 2.2 fusion.145
  38.1 1.9 fusion.158
  40.0 3.3 concatenate.80
  44.4 3.4 concatenate.81
  48.8 3.3 concatenate.82
  53.1 3.4 concatenate.83
  57.4 4.2 concatenate.84
  61.7 2.1 fusion.14
  63.7 4.2 concatenate.85
  68.0 2.1 fusion.13
  70.0 4.2 concatenate.86
  74.3 2.1 fusion.12
  76.3 4.2 concatenate.87
  80.6 2.0 fusion.11
  82.7 1.4 fusion.10
  84.0 1.4 fusion.9
  86.8 1.4 fusion.7
  90.8 1.4 fusion.4
  94.5 214.7 %all-reduce.8.cloned.1.call-done = f32[128,128]{1,0:T(8,128)} async-done(((f32[128,128]{1,0:T(8,128)}), f32[128,128]{1,0:T(8,128)}) %all-reduce.8.cloned.1.call-update) | async-done | bytes 65552 | tf_op jit(solution)/shard_map/psum | solution.py:79
  311.0 11.7 %cholesky.100 = f32[128,128]{1,0:T(8,128)S(1)} custom-call(f32[128,128]{1,0:T(8,128)S(1)} %fusion.73), custom_call_target="Cholesky" | custom-call | tf_op jit(solution)/shard_map/jit(cholesky)/cholesky | solution.py:91
  324.0 10.4 %custom-call.44 = f32[1,128,128]{1,2,0:T(8,128)} custom-call(f32[1,128,128]{2,1,0:T(8,128)S(1)} %fusion.62), custom_call_target="InvertDiagBlocksLowerTriangular" | custom-call | tf_op jit(solution)/shard_map/jit(_cho_solve)/triangular_solve | solution.py:96
  334.5 1.6 slice.1801
  340.9 9.6 %reduce-scatter.3.cloned.1.call-done = f32[1,432,432]{2,1,0:T(8,128)} async-done(((f32[8,432,432]{2,1,0:T(8,128)}), f32[1,432,432]{2,1,0:T(8,128)}) %reduce-scatter.3.cloned.1.call-update) | async-done | bytes 746512 | tf_op jit(solution)/shard_map/reduce_scatter | solution.py:83
  352.1 268.3 %all-reduce.10.cloned.1.call-done = (f32[1,432,432]{2,1,0:T(8,128)}, f32[1,432,128]{2,1,0:T(8,128)}) async-done(((f32[1,432,432]{2,1,0:T(8,128)}, f32[1,432,128]{2,1,0:T(8,128)}), (f32[1,432,432]{2,1,0:T(8,128)}, f32[1,432,128]{2,1,0:T(8,128)})) %all-reduce.10.cloned.1.call-update) | async-done | bytes 967696 | tf_op jit(solution)/shard_map/psum | solution.py:81
  621.4 1.4 bitcast_add_fusion.1
  623.3 12.1 %cholesky.109 = f32[128,128]{1,0:T(8,128)S(1)} custom-call(f32[128,128]{1,0:T(8,128)S(1)} %cholesky.264), custom_call_target="Cholesky" | custom-call | tf_op jit(solution)/shard_map/jit(cholesky)/cholesky | solution.py:93
  636.2 9.8 %custom-call.45 = f32[1,128,128]{1,2,0:T(8,128)S(1)} custom-call(f32[1,128,128]{2,1,0:T(8,128)S(1)} %get-tuple-element.273), custom_call_target="InvertDiagBlocksLowerTriangular" | custom-call | tf_op jit(solution)/shard_map/jit(cholesky)/cholesky | solution.py:93
  648.6 11.7 %cholesky.212 = f32[128,128]{1,0:T(8,128)S(1)} custom-call(f32[128,128]{1,0:T(8,128)S(1)} %cholesky.268), custom_call_target="Cholesky" | custom-call | tf_op jit(solution)/shard_map/jit(cholesky)/cholesky | solution.py:93
  661.0 9.8 %custom-call.46 = f32[1,128,128]{1,2,0:T(8,128)S(1)} custom-call(f32[1,128,128]{2,1,0:T(8,128)S(1)} %get-tuple-element.270), custom_call_target="InvertDiagBlocksLowerTriangular" | custom-call | tf_op jit(solution)/shard_map/jit(cholesky)/cholesky | solution.py:93
  672.3 11.9 %cholesky.233 = f32[128,128]{1,0:T(8,128)S(1)} custom-call(f32[128,128]{1,0:T(8,128)S(1)} %cholesky.273), custom_call_target="Cholesky" | custom-call | tf_op jit(solution)/shard_map/jit(cholesky)/cholesky | solution.py:93
  684.8 9.8 %custom-call.47 = f32[1,128,128]{1,2,0:T(8,128)S(1)} custom-call(f32[1,128,128]{2,1,0:T(8,128)S(1)} %get-tuple-element.267), custom_call_target="InvertDiagBlocksLowerTriangular" | custom-call | tf_op jit(solution)/shard_map/jit(cholesky)/cholesky | solution.py:93
  695.8 4.4 cholesky.253
  703.5 6.1 while.1
  704.2 1.4 bitcast_dynamic-update-slice_fusion.2
  706.2 1.4 bitcast_dynamic-update-slice_fusion.2
  708.2 1.4 bitcast_dynamic-update-slice_fusion.2
  709.8 39.3 %custom-call.48 = f32[4,128,128]{1,2,0:T(8,128)S(1)} custom-call(f32[4,128,128]{2,1,0:T(8,128)S(1)} %pad_maximum_fusion.1), custom_call_target="InvertDiagBlocksLowerTriangular" | custom-call | tf_op jit(solution)/shard_map/jit(_cho_solve)/triangular_solve | solution.py:95
  754.6 32.0 %psum.31 = f32[]{:T(128)} all-reduce(f32[]{:T(128)} %get-tuple-element.278), channel_id=1, replica_groups=mesh['space'=32,'fac'=8] {'fac'}, use_global_device_ids=true, to_apply=%region_16.17 | all-reduce | flops 1 | bytes 8 | tf_op jit(solution)/shard_map/psum | solution.py:97
  (147 shorter events, 44.4 us)
Async XLA Ops:
  8.0 7.6 copy-start
  8.0 5.6 copy-start.1
  8.0 301.1 %all-reduce.8.cloned.1.call-start = ((), (), s32[]{:S(2)}) async-start(), calls=%async_computation.2 | async-start | bytes 131072 | tf_op jit(solution)/shard_map/psum | solution.py:79
  9.9 330.9 %reduce-scatter.5.cloned.1.call-start = ((), (), s32[]{:S(2)}) async-start(), calls=%async_computation.4 | async-start | bytes 1990656 | tf_op jit(solution)/shard_map/reduce_scatter | solution.py:84
  11.0 3.8 collective-permute-start
  12.3 3.3 collective-permute-start.1
  38.1 1.9 copy-start.6
  44.4 4.4 copy-start.11
  82.6 267.9 %reduce-scatter.3.cloned.1.call-start = ((), (), s32[]{:S(2)}) async-start(), calls=%async_computation.3 | async-start | bytes 7962624 | tf_op jit(solution)/shard_map/reduce_scatter | solution.py:83
  85.4 2.7 copy-start.2
  86.8 2.7 copy-start.3
  88.1 2.7 copy-start.4
  89.5 2.7 copy-start.5
  93.6 242.6 %copy-start.10 = (bf16[27,128,128]{2,1,0:T(8,128)(2,1)S(1)}, bf16[27,128,128]{2,1,0:T(8,128)(2,1)}, u32[]{:S(2)}) copy-start(bf16[27,128,128]{2,1,0:T(8,128)(2,1)} %param.5) | copy-start | bytes 2654212
  93.6 526.9 %all-reduce.10.cloned.1.call-start = ((), (), s32[]{:S(2)}) async-start(), calls=%async_computation.5 | async-start | bytes 2211840 | tf_op jit(solution)/shard_map/psum | solution.py:81
  340.0 10.5 %copy-start.12 = (bf16[2,16,16,128]{3,2,1,0:T(8,128)(2,1)S(1)}, bf16[2,16,16,128]{3,2,1,0:T(8,128)(2,1)}, u32[]{:S(2)}) copy-start(bf16[2,16,16,128]{3,2,1,0:T(8,128)(2,1)} %slice.1801) | copy-start | bytes 393220
  621.4 1.7 copy-start.7
  623.3 12.9 %copy-start.8 = (f32[432,432]{1,0:T(8,128)}, f32[432,432]{1,0:T(8,128)S(1)}, u32[]{:S(2)}) copy-start(f32[432,432]{1,0:T(8,128)S(1)} %fusion.25) | copy-start | bytes 2239492
  648.5 55.0 %copy-start.15 = (f32[3,128,128]{2,1,0:T(8,128)S(1)}, f32[3,128,128]{2,1,0:T(8,128)}, u32[]{:S(2)}) copy-start(f32[3,128,128]{2,1,0:T(8,128)} %custom-call.51) | copy-start | bytes 589828
  672.2 37.4 %copy-start.13 = (f32[128,80]{1,0:T(8,128)S(1)}, f32[128,80]{1,0:T(8,128)}, u32[]{:S(2)}) copy-start(f32[128,80]{1,0:T(8,128)} %pad_convert_fusion) | copy-start | bytes 122884
  709.7 43.3 %copy-start.14 = (f32[1,128,128]{1,2,0:T(8,128)S(1)}, f32[1,128,128]{1,2,0:T(8,128)}, u32[]{:S(2)}) copy-start(f32[1,128,128]{1,2,0:T(8,128)} %custom-call.44) | copy-start | bytes 196612
  749.4 4.1 copy-start.9
Sparse Core Ops, SparseCore 0:
  14.4 294.7 all-reduce.7
Sparse Core Ops, SparseCore 1:
  82.7 99.6 reduce-scatter.4
  186.6 163.9 reduce-scatter.2
  353.3 267.1 all-reduce.9
where the time goes:
time: 806 us; the launch traced here: 796 us
  waiting for transfers between devices  494 us (61%)
  other arithmetic  142 us (18%)
  local copies, waits for them, and re-layouts  64 us (8%)
  matrix products  41.1 us (5%)
  blocking collectives  32 us (4%)
  between operations  19.9 us (2%)
    psum x1, waiting for transfers between devices, on_device(): summed = lax.psum((grams, grads), 'space')  268 us
    psum x1, waiting for transfers between devices, on_device(): cot_total = lax.psum(cot_gram, ('space', 'fac'))  215 us
    another operation x15, other arithmetic, on_device(): left_chol = jnp.linalg.cholesky(left_mat)  72.3 us
    another operation x7, other arithmetic, on_device(): half = jax.scipy.linalg.cho_solve((left_chol, True), scaled)  40.2 us
    psum x1, blocking collectives, on_device(): total = lax.psum(jnp.sum(raw * scaled), 'fac')  32 us
    concatenate x8, local copies, waits for them, and re-layouts, local_stats(): patch = jnp.concatenate(pieces, axis=1)  30.3 us
    slice x13, local copies, waits for them, and re-layouts, local_stats(): window(padded_in, shift, extent)[..., lower:lower + width]  25.1 us
  transfers between devices with their start and end apart: 6, of which 4 were waited for; matrix products, arithmetic and copies ran while one was open for 14% of the time, Pallas kernels for 0%

commit v1 on v0

--- a/solution.py
+++ b/solution.py
@@ -76,7 +76,7 @@
         rows = window(padded_cot, back, extent).reshape(cells, channels)
         in_grad = in_grad + jnp.dot(rows, kernel[tap_index].T, preferred_element_type=jnp.float32)
     in_grad = in_grad.astype(jnp.bfloat16).reshape(activations.shape)
-    cot_total = lax.psum(cot_gram, ("space", "fac"))
+    cot_total = jnp.sum(lax.all_gather(cot_gram, axis_name=("space", "fac")), axis=0)
     grams, grads = local_stats(padded_in, rows_cot, extent, groups)
     summed = lax.psum((grams, grads), "space")
     owned = (

time: 806 us -> 1170 us (1.45)
  waiting for transfers between devices: 494 us -> 854 us
    all_gather x0 -> x1, waiting for transfers between devices: none -> 336 us  [on_device(): lax.all_gather(cot_gram, axis_name=('space', 'fac'))]
    psum x1 -> x0, waiting for transfers between devices: 215 us -> none  [on_device(): cot_total = lax.psum(cot_gram, ('space', 'fac'))]
    reduce_scatter x1, waiting for transfers between devices: 9.63 us -> 168 us  [on_device(): lax.psum_scatter(summed[0], 'fac', scatter_dimension=0, tiled=True)]
    reduce_scatter x1, waiting for transfers between devices: 0.03 us -> 87.7 us  [on_device(): lax.psum_scatter(summed[1], 'fac', scatter_dimension=0, tiled=True)]
  transfers between devices with their start and end apart: 6 -> 6, of which waited for: 4 -> 4; matrix products, arithmetic and copies ran while one was open for 14% -> 13% of each run, Pallas kernels for 0% -> 0%
where the time goes in v1:
time: 1170 us; the launch traced here: 1160 us
  waiting for transfers between devices  854 us (73%)
  other arithmetic  145 us (12%)
  local copies, waits for them, and re-layouts  64.9 us (6%)
  matrix products  40.1 us (3%)
  blocking collectives  28.6 us (2%)
  between operations  19.2 us (2%)
    all_gather x1, waiting for transfers between devices, on_device(): lax.all_gather(cot_gram, axis_name=('space', 'fac'))  336 us
    psum x1, waiting for transfers between devices, on_device(): summed = lax.psum((grams, grads), 'space')  262 us
    reduce_scatter x1, waiting for transfers between devices, on_device(): lax.psum_scatter(summed[0], 'fac', scatter_dimension=0, tiled=True)  168 us
    reduce_scatter x1, waiting for transfers between devices, on_device(): lax.psum_scatter(summed[1], 'fac', scatter_dimension=0, tiled=True)  87.7 us
    another operation x15, other arithmetic, on_device(): left_chol = jnp.linalg.cholesky(left_mat)  72 us
    another operation x7, other arithmetic, on_device(): half = jax.scipy.linalg.cho_solve((left_chol, True), scaled)  40.2 us
    concatenate x8, local copies, waits for them, and re-layouts, local_stats(): patch = jnp.concatenate(pieces, axis=1)  30.2 us
    psum x1, blocking collectives, on_device(): total = lax.psum(jnp.sum(raw * scaled), 'fac')  28.6 us
  transfers between devices with their start and end apart: 6, of which 4 were waited for; matrix products, arithmetic and copies ran while one was open for 13% of the time, Pallas kernels for 0%

profile of v1, /device:TPU:0, one launch (start us, length us, event | category | flops | bytes accessed | tf_op | source)
XLA Modules:
  0.0 1155.4 jit_solution(13497837302150111990)
XLA Ops:
  11.7 2.7 fusion.161
  15.6 1.7 fusion.151
  17.3 1.8 fusion.155
  19.1 2.2 fusion.153
  21.3 2.3 fusion.149
  23.5 2.3 fusion.150
  25.8 2.2 fusion.147
  28.1 2.3 fusion.154
  30.3 2.2 fusion.148
  32.5 2.2 fusion.152
  34.8 2.2 fusion.146
  37.1 1.9 fusion.159
  39.0 3.3 concatenate.80
  43.3 3.4 concatenate.81
  47.7 3.3 concatenate.82
  52.1 3.4 concatenate.83
  56.4 4.2 concatenate.84
  60.6 2.0 fusion.14
  62.7 4.2 concatenate.85
  66.9 2.0 fusion.13
  68.9 4.2 concatenate.86
  73.2 2.0 fusion.12
  75.2 4.2 concatenate.87
  79.4 2.0 fusion.11
  81.5 1.4 fusion.10
  82.9 1.4 fusion.9
  85.6 1.4 fusion.7
  89.7 1.4 fusion.4
  92.5 87.7 %reduce-scatter.5.cloned.1.call-done = f32[1,432,128]{2,1,0:T(8,128)} async-done(((f32[8,432,128]{2,1,0:T(8,128)}), f32[1,432,128]{2,1,0:T(8,128)}) %reduce-scatter.5.cloned.1.call-update) | async-done | bytes 221200 | tf_op jit(solution)/shard_map/reduce_scatter | solution.py:84
  180.1 168.3 %reduce-scatter.3.cloned.1.call-done = f32[1,432,432]{2,1,0:T(8,128)} async-done(((f32[8,432,432]{2,1,0:T(8,128)}), f32[1,432,432]{2,1,0:T(8,128)}) %reduce-scatter.3.cloned.1.call-update) | async-done | bytes 746512 | tf_op jit(solution)/shard_map/reduce_scatter | solution.py:83
  357.6 262.1 %all-reduce.7.cloned.1.call-done = (f32[1,432,432]{2,1,0:T(8,128)}, f32[1,432,128]{2,1,0:T(8,128)}) async-done(((f32[1,432,432]{2,1,0:T(8,128)}, f32[1,432,128]{2,1,0:T(8,128)}), (f32[1,432,432]{2,1,0:T(8,128)}, f32[1,432,128]{2,1,0:T(8,128)})) %all-reduce.7.cloned.1.call-update) | async-done | bytes 967696 | tf_op jit(solution)/shard_map/psum | solution.py:81
  621.7 11.7 %cholesky.109 = f32[128,128]{1,0:T(8,128)S(1)} custom-call(f32[128,128]{1,0:T(8,128)S(1)} %cholesky.264), custom_call_target="Cholesky" | custom-call | tf_op jit(solution)/shard_map/jit(cholesky)/cholesky | solution.py:93
  633.4 9.8 custom-call.45
  645.8 12.1 %cholesky.212 = f32[128,128]{1,0:T(8,128)S(1)} custom-call(f32[128,128]{1,0:T(8,128)S(1)} %cholesky.268), custom_call_target="Cholesky" | custom-call | tf_op jit(solution)/shard_map/jit(cholesky)/cholesky | solution.py:93
  657.9 9.8 custom-call.46
  669.2 11.7 %cholesky.233 = f32[128,128]{1,0:T(8,128)S(1)} custom-call(f32[128,128]{1,0:T(8,128)S(1)} %cholesky.273), custom_call_target="Cholesky" | custom-call | tf_op jit(solution)/shard_map/jit(cholesky)/cholesky | solution.py:93
  681.0 9.8 custom-call.47
  692.0 4.4 cholesky.253
  701.5 6.1 while.1
  702.3 1.4 bitcast_dynamic-update-slice_fusion.2
  704.2 1.4 bitcast_dynamic-update-slice_fusion.2
  706.2 1.4 bitcast_dynamic-update-slice_fusion.2
  707.6 39.3 %custom-call.48 = f32[4,128,128]{1,2,0:T(8,128)S(1)} custom-call(f32[4,128,128]{2,1,0:T(8,128)S(1)} %pad_maximum_fusion.1), custom_call_target="InvertDiagBlocksLowerTriangular" | custom-call | tf_op jit(solution)/shard_map/jit(_cho_solve)/triangular_solve | solution.py:95
  750.9 335.8 %all-gather.3.cloned.1.call-done = f32[32768,128]{1,0:T(8,128)} async-done(((f32[128,128]{1,0:T(8,128)}), f32[32768,128]{1,0:T(8,128)}) %all-gather.3.cloned.1.call-update) | async-done | bytes 16777232 | tf_op jit(solution)/shard_map/all_gather | solution.py:79
  1086.7 6.6 reduce_sum.18
  1093.5 11.7 %cholesky.100 = f32[128,128]{1,0:T(8,128)S(1)} custom-call(f32[128,128]{1,0:T(8,128)S(1)} %fusion.74), custom_call_target="Cholesky" | custom-call | tf_op jit(solution)/shard_map/jit(cholesky)/cholesky | solution.py:91
  1106.5 9.8 custom-call.44
  1118.0 28.6 %psum.23 = f32[]{:T(128)} all-reduce(f32[]{:T(128)} %get-tuple-element.278), channel_id=1, replica_groups=mesh['space'=32,'fac'=8] {'fac'}, use_global_device_ids=true, to_apply=%region_16.17 | all-reduce | flops 1 | bytes 8 | tf_op jit(solution)/shard_map/psum | solution.py:97
  (145 shorter events, 42.8 us)
Async XLA Ops:
  8.0 6.4 copy-start
  8.0 6.4 copy-start.1
  8.0 172.1 %reduce-scatter.5.cloned.1.call-start = ((), (), s32[]{:S(2)}) async-start(), calls=%async_computation.4 | async-start | bytes 1990656 | tf_op jit(solution)/shard_map/reduce_scatter | solution.py:84
  9.1 5.3 collective-permute-start
  10.4 4.0 collective-permute-start.1
  37.1 1.9 copy-start.6
  43.3 4.4 copy-start.11
  81.5 267.0 %reduce-scatter.3.cloned.1.call-start = ((), (), s32[]{:S(2)}) async-start(), calls=%async_computation.3 | async-start | bytes 7962624 | tf_op jit(solution)/shard_map/reduce_scatter | solution.py:83
  84.3 2.7 copy-start.2
  85.6 2.7 copy-start.3
  87.0 2.7 copy-start.4
  88.3 2.7 copy-start.5
  92.4 527.3 %all-reduce.7.cloned.1.call-start = ((), (), s32[]{:S(2)}) async-start(), calls=%async_computation.5 | async-start | bytes 2211840 | tf_op jit(solution)/shard_map/psum | solution.py:81
  348.4 2.9 copy-start.10
  348.5 738.2 %all-gather.3.cloned.1.call-start = ((), (), s32[]{:S(2)}) async-start(), calls=%async_computation.2 | async-start | bytes 16842752 | tf_op jit(solution)/shard_map/all_gather | solution.py:79
  619.8 1.7 copy-start.7
  621.6 11.8 %copy-start.8 = (f32[432,432]{1,0:T(8,128)}, f32[432,432]{1,0:T(8,128)S(1)}, u32[]{:S(2)}) copy-start(f32[432,432]{1,0:T(8,128)S(1)} %fusion.25) | copy-start | bytes 2239492
  645.8 55.6 %copy-start.12 = (f32[128,80]{1,0:T(8,128)S(1)}, f32[128,80]{1,0:T(8,128)}, u32[]{:S(2)}) copy-start(f32[128,80]{1,0:T(8,128)} %pad_convert_fusion) | copy-start | bytes 122884
  657.9 43.6 %copy-start.13 = (f32[3,128,128]{2,1,0:T(8,128)S(1)}, f32[3,128,128]{2,1,0:T(8,128)}, u32[]{:S(2)}) copy-start(f32[3,128,128]{2,1,0:T(8,128)} %custom-call.51) | copy-start | bytes 589828
  691.0 56.0 %copy-start.9 = (f32[1,432,128]{2,1,0:T(8,128)S(1)}, f32[1,432,128]{2,1,0:T(8,128)}, u32[]{:S(2)}) copy-start(f32[1,432,128]{2,1,0:T(8,128)} %get-tuple-element.19) | copy-start | bytes 663556
Sparse Core Ops, SparseCore 0:
  81.6 98.4 reduce-scatter.4
  184.4 163.9 reduce-scatter.2
  351.4 268.3 all-reduce.6
Sparse Core Ops, SparseCore 1:
  350.8 735.8 all-gather.2
